TPU v7x, 128 devices: a whole 4x4x4 slice. The times are simulated.
128 devices in a mesh: vrow: 8 (over z, core), vcol: 16 (over x, y).
Axes of the slice: x: 4, y: 4, z: 4, core: 2. Of those that a mesh axis runs over, the one named last changes fastest.
Arguments:
- pair_amps: bfloat16 [768, 32768], P('vrow', 'vcol'), may hold values from -6 to 6
- integrals: bfloat16 [8, 16, 512, 128, 128], P('vrow', 'vcol'), may hold values from -0.046875 to 0.046875
- block_index: int32 [8, 16, 512], P('vrow', 'vcol'), may hold values from 0 to 511, as said below
- block_count: int32 [8, 16], P('vrow', 'vcol'), may hold values from 64 to 512, as said below
Outputs:
- ladder: bfloat16 [768, 32768], P('vcol', 'vrow')
Inputs may be any that keep to these rules, and one draw needn't show every extreme that they name: Within one device group (g, h) the entries of block_index are distinct, a permutation of all 512 tile pairs. `block_count`: some device group holds all 512 slots live.
All inputs are finite; a program needn't handle non-finite values.
Results may differ from a plain program's by a relative error of at most 0.001.
Values may be sent and summed in bfloat16 or wider, within the bound.
A program may use at most 128 MiB of HBM per device.

v0:
```python
import jax
import jax.numpy as jnp
from jax import lax
from jax.sharding import PartitionSpec as P


def shifted(array, axis, by):
    size = lax.axis_size(axis)
    return lax.ppermute(array, axis, [(i, (i + by) % size) for i in range(size)])


def per_device(pair_amps, integrals, block_index, block_count):
    tile_size = integrals.shape[-1]
    blocks = integrals[0, 0]
    slot_index = block_index[0, 0]
    live_count = block_count[0, 0]
    slot_total = blocks.shape[0]
    cd_tiles = pair_amps.shape[1] // tile_size
    ab_tiles = slot_total // cd_tiles
    slot_ids = jnp.arange(slot_total, dtype=jnp.int32)
    keep_mask = slot_ids < live_count
    selector = jnp.logical_and(slot_index[None, :] == slot_ids[:, None], keep_mask[None, :]).astype(
        jnp.bfloat16
    )
    flat_blocks = blocks.reshape(slot_total, tile_size * tile_size)
    placed = jnp.dot(selector, flat_blocks, preferred_element_type=jnp.float32).astype(jnp.bfloat16)
    placed = placed.reshape(ab_tiles, cd_tiles, tile_size, tile_size)
    dense_weights = jnp.transpose(placed, (1, 2, 0, 3)).reshape(
        cd_tiles * tile_size, ab_tiles * tile_size
    )
    partial_value = jnp.dot(
        lax.all_gather(pair_amps, "vrow", axis=0, tiled=True),
        dense_weights,
        preferred_element_type=jnp.float32,
    )
    vcol_size = lax.axis_size("vcol")
    summed = lax.psum_scatter(partial_value, "vcol", scatter_dimension=0, tiled=True)
    mirror_part = shifted(summed, "vcol", vcol_size // 2)
    result = summed - mirror_part
    return result.astype(jnp.bfloat16)


def solution(mesh):
    placed = (
        P("vrow", "vcol"),
        P("vrow", "vcol", None, None, None),
        P("vrow", "vcol", None),
        P("vrow", "vcol"),
    )
    return jax.shard_map(
        per_device, mesh=mesh, in_specs=placed, out_specs=P("vcol", "vrow"), check_vma=False
    )
```

profile of v0, /device:TPU:0, one launch (start us, length us, event | category | flops | bytes accessed | tf_op | source)
XLA Modules:
  0.0 218.6 jit_solution(2575144080358008372)
XLA Ops:
  6.5 0.0 all-gather.2.cloned.1.call-start
  6.5 0.7 all-gather.2.cloned.1.call-update
  7.3 0.0 reduce-scatter.4.cloned.1.call-start
  8.0 22.3 %fusion.5 = bf16[64,8,128,128]{3,1,2,0:T(8,128)(2,1)} fusion(bf16[64,8,128,128]{3,2,1,0:T(8,128)(2,1)} %bitcast.28, s32[512]{0:T(512)} %bitcast.29, pred[512]{0:T(512)(128)(4,1)S(1)} %iota_compare_fusion.1), kind=kOutput, calls=%fused_computation.6 | convolution fusion | flops 8598847488 | bytes 33556992 | tf_op jit(solution)/shard_map/dot_general | solution.py:26
  30.3 10.0 %copy.18 = bf16[64,8,128,128]{3,2,1,0:T(8,128)(2,1)S(1)} copy(bf16[64,8,128,128]{3,1,2,0:T(8,128)(2,1)} %fusion.5) | data formatting | bytes 33554432
  40.3 11.6 %copy.12 = bf16[32,16,128,128]{3,0,2,1:T(8,128)(2,1)} copy(bf16[32,16,128,128]{3,2,1,0:T(8,128)(2,1)S(1)} %bitcast.26) | data formatting | bytes 33554432 | tf_op jit(solution)/shard_map/reshape | solution.py:27
  51.9 0.0 all-gather.2.cloned.1.call-done
  51.9 27.6 %fusion.8 = f32[768,4096]{0,1:T(8,128)} fusion(bf16[768,2048]{1,0:T(8,128)(2,1)} %all-gather.2.cloned.1.call-done, bf16[256,8,32,128]{3,2,1,0:T(8,128)(2,1)} %bitcast.27), kind=kOutput, calls=%fused_computation.7 | convolution fusion | flops 12884901888 | bytes 32505856 | tf_op jit(solution)/shard_map/dot_general | solution.py:31
  79.5 12.6 %copy.15 = f32[768,4096]{1,0:T(8,128)} copy(f32[768,4096]{0,1:T(8,128)} %fusion.8) | data formatting | bytes 25165824
  92.2 0.0 reduce-scatter.4.cloned.1.call-update
  92.2 96.9 %reduce-scatter.4.cloned.1.call-done = f32[48,4096]{1,0:T(8,128)} async-done(((f32[768,4096]{1,0:T(8,128)}), f32[48,4096]{1,0:T(8,128)}) %reduce-scatter.4.cloned.1.call-update) | async-done | bytes 786448 | tf_op jit(solution)/shard_map/reduce_scatter | solution.py:37
  189.1 2.3 %collective-permute-start = (f32[48,4096]{1,0:T(8,128)}, f32[48,4096]{1,0:T(8,128)S(1)}, u32[]{:S(2)}, u32[]{:S(2)}) collective-permute-start(f32[48,4096]{1,0:T(8,128)} %reduce-scatter.4.cloned.1.call-done), channel_id=1, source_target_pairs={{0,8},{1,9},{2,10},{3,11},{4,12},{5,13},{6,14},{7,15},{8,0},{9,1},... | collective-permute-start | bytes 2359304 | tf_op jit(solution)/shard_map/ppermute | solution.py:9
  191.4 18.4 %collective-permute-done = f32[48,4096]{1,0:T(8,128)S(1)} collective-permute-done((f32[48,4096]{1,0:T(8,128)}, f32[48,4096]{1,0:T(8,128)S(1)}, u32[]{:S(2)}, u32[]{:S(2)}) %collective-permute-start) | collective-permute-done | bytes 786464 | tf_op jit(solution)/shard_map/ppermute | solution.py:9
  209.8 1.9 subtract_convert_fusion
  (1 shorter events, 0.0 us)
Async XLA Ops:
  6.5 45.3 %all-gather.2.cloned.1.call-start = ((), (), s32[]{:S(2)}) async-start(), calls=%async_computation.1 | async-start | bytes 3538944 | tf_op jit(solution)/shard_map/all_gather | solution.py:32
  7.3 181.9 %reduce-scatter.4.cloned.1.call-start = ((), (), s32[]{:S(2)}) async-start(), calls=%async_computation.2 | async-start | bytes 13369344 | tf_op jit(solution)/shard_map/reduce_scatter | solution.py:37
  189.1 20.7 %collective-permute-start = (f32[48,4096]{1,0:T(8,128)}, f32[48,4096]{1,0:T(8,128)S(1)}, u32[]{:S(2)}, u32[]{:S(2)}) collective-permute-start(f32[48,4096]{1,0:T(8,128)} %reduce-scatter.4.cloned.1.call-done), channel_id=1, source_target_pairs={{0,8},{1,9},{2,10},{3,11},{4,12},{5,13},{6,14},{7,15},{8,0},{9,1},... | collective-permute-start | bytes 2359304 | tf_op jit(solution)/shard_map/ppermute | solution.py:9
Sparse Core Ops, SparseCore 0:
  9.0 30.4 all-gather.1
  92.3 96.7 reduce-scatter.3
where the time goes:
time: 219 us
  waiting for transfers between devices  116 us (53%)
  matrix products  50 us (23%)
  local copies, waits for them, and re-layouts  34.2 us (16%)
  between operations  14.1 us (6%)
  starting transfers between devices  2.32 us (1%)
    reduce_scatter x1, waiting for transfers between devices, per_device(): lax.psum_scatter(partial_value, 'vcol', scatter_dimension=0, tiled=True)  96.9 us
    dot_general x1, matrix products, per_device(): jnp.dot(lax.all_gather(pair_amps, 'vrow', axis=0, tiled=True), dense_weig...  27.6 us
    unnamed x2, local copies, waits for them, and re-layouts  22.6 us
    dot_general x1, matrix products, per_device(): jnp.dot(selector, flat_blocks, preferred_element_type=jnp.float32)  22.3 us
    ppermute x1, waiting for transfers between devices, shifted(): lax.ppermute(array, axis, [(i, (i + by) % size) for i in range(size)])  18.4 us
    reshape x1, local copies, waits for them, and re-layouts, per_device(): placed = placed.reshape(ab_tiles, cd_tiles, tile_size, tile_size)  11.6 us
  transfers between devices with their start and end apart: 3, of which 2 were waited for; matrix products, arithmetic and copies ran while one was open for 20% of the time, Pallas kernels for 0%

commit v1 on v0

v1 whole, which is shorter than its diff:
```python
import jax
import jax.numpy as jnp
from jax import lax
from jax.experimental import pallas as pl
from jax.experimental.pallas import tpu as pltpu
from jax.sharding import PartitionSpec as P

MESH = pl.DeviceIdType.MESH
F32 = jnp.float32
TILE = 128
SLOTS = 512
CD = 16
DEPTH = CD * TILE
PASSES = 3
COLS = 512
UNITS = 24
PER_PASS = 8
LEVELS = 32766.0
PARTS = 16


def dims_of(rotation):
    return [(rotation + k) % 4 for k in range(4)]


def mask_of(position, dims):
    mask = 0
    for k in range(4):
        mask |= ((position >> (3 - k)) & 1) << dims[k]
    return mask


def kernel(
    inv, amps, w_hbm, out, wv, a, d, s0, s1, s2, s3, r0, r1, r2, r3, held,
    wsem, asem, gsend, grecv, ssend, srecv,
):
    vrow, vcol = lax.axis_index("vrow"), lax.axis_index("vcol")
    z, core = vrow // 2, vrow % 2
    x, y = vcol // 4, vcol % 4
    sent, got = [s0, s1, s2, s3], [r0, r1, r2, r3]

    per = SLOTS // PARTS

    def load_part(c):
        part = pl.ds(c * per, per)
        return pltpu.make_async_copy(w_hbm.at[part], wv.at[part], wsem.at[c])

    def load_rows(s, i):
        return pltpu.make_async_copy(
            amps.at[pl.ds(48 * i + 16 * s, 16)],
            a.at[s, pl.ds(32 * vrow + 16 * i, 16)],
            asem.at[2 * s + i],
        )

    for s in range(PASSES):
        for i in range(2):
            load_rows(s, i).start()
    for c in range(PARTS):
        load_part(c).start()

    above, below = (vrow + 2) % 8, (vrow + 6) % 8
    sibling = 2 * z + 1 - core
    partner = [
        (x + 1 - 2 * (x % 2)) * 4 + y,
        x * 4 + (y + 1 - 2 * (y % 2)),
        (3 - x) * 4 + y,
        x * 4 + (3 - y),
    ]
    opposite = ((x + 2) % 4) * 4 + y

    barrier = pltpu.get_barrier_semaphore()
    peers = [(above, vcol), (below, vcol), (sibling, vcol)]
    peers += [(vrow, p) for p in partner] + [(vrow, opposite)]
    for peer in peers:
        pl.semaphore_signal(barrier, inc=1, device_id=peer, device_id_type=MESH)
    wv[SLOTS] = jnp.zeros((TILE, TILE), jnp.bfloat16)
    for s in range(PASSES):
        for i in range(2):
            load_rows(s, i).wait()
    pl.semaphore_wait(barrier, len(peers))

    def piece(s, first, rows, target, kind):
        ref = a.at[s, pl.ds(pl.multiple_of(first, 16), rows)]
        return pltpu.make_async_remote_copy(
            src_ref=ref, dst_ref=ref,
            send_sem=gsend.at[s, kind], recv_sem=grecv.at[s, kind],
            device_id=(target, vcol), device_id_type=MESH,
        )

    own, low, high, far = 32 * vrow, 32 * below, 32 * above, 32 * ((vrow + 4) % 8)
    near = 32 * sibling

    def gather_copy(s, kind):
        first, rows, target = [
            (own, 32, above), (own, 32, below), (own, 32, sibling),
            (low, 16, above), (low, 32, sibling),
            (high + 16, 16, below), (high, 32, sibling),
            (far, 32, sibling),
        ][kind]
        return piece(s, first, rows, target, kind)

    def arrived(s, kind):
        first, rows = [
            (low, 32), (high, 32), (near, 32), (far, 16),
            (32 * ((sibling + 6) % 8), 32), (far + 16, 16),
            (32 * ((sibling + 2) % 8), 32), (32 * ((sibling + 4) % 8), 32),
        ][kind]
        piece(s, first, rows, sibling, kind).wait_recv()

    def gather_start(s):
        for kind in (0, 1, 2):
            gather_copy(s, kind).start()

    def gather_forward(s):
        arrived(s, 0)
        gather_copy(s, 3).start()
        gather_copy(s, 4).start()
        arrived(s, 1)
        gather_copy(s, 5).start()
        gather_copy(s, 6).start()

    def gather_last(s):
        arrived(s, 3)
        arrived(s, 5)
        gather_copy(s, 7).start()

    def gather_end(s):
        for kind in (2, 4, 6, 7):
            arrived(s, kind)

    xa, xb = ((x + 1) // 2) % 2, x // 2
    ya, yb = ((y + 1) // 2) % 2, y // 2
    place = []
    for m in range(16):
        ta, tya = (xa + (m & 1)) % 2, (ya + ((m >> 1) & 1)) % 2
        tb, tyb = (xb + ((m >> 2) & 1)) % 2, (yb + ((m >> 3) & 1)) % 2
        group = 4 * ((ta + tb) % 2) + 2 * tyb + (tya + tyb) % 2
        place.append((pl.multiple_of(16 * group, 16), pl.multiple_of(256 * tb, 256)))

    def share(u, position, dims):
        row, col = place[mask_of(position, dims)]
        return d.at[u, pl.ds(row, 16), pl.ds(col, 256)]

    def exchange(u, k, dims):
        return pltpu.make_async_remote_copy(
            src_ref=sent[k].at[u], dst_ref=got[k].at[u],
            send_sem=ssend.at[u, k], recv_sem=srecv.at[u, k],
            device_id=(vrow, partner[dims[k]]), device_id_type=MESH,
        )

    def pack(u, k, values):
        most = jnp.abs(values[0])
        for value in values[1:]:
            most = jnp.maximum(most, jnp.abs(value))
        most = jnp.maximum(jnp.max(most, axis=0, keepdims=True), 1e-30)
        code = jnp.ceil(jnp.log(most) * 256.0)
        factor = jnp.exp(code * (-1.0 / 256.0)) * LEVELS
        for n, value in enumerate(values):
            q = jnp.round(value * factor).astype(jnp.int32)
            sent[k][u, 16 * n : 16 * n + 16] = q.astype(jnp.int16)
        n = len(values)
        wide = jnp.broadcast_to(code, (16, 256)).astype(jnp.int32)
        sent[k][u, 16 * n : 16 * n + 16] = wide.astype(jnp.int16)

    def unpack(u, k, n):
        count = 8 >> k
        code = got[k][u, 16 * count : 16 * count + 16].astype(jnp.int32).astype(F32)
        factor = jnp.exp(code * (1.0 / 256.0)) * (1.0 / LEVELS)
        q = got[k][u, 16 * n : 16 * n + 16].astype(jnp.int32).astype(F32)
        return q * factor

    def multiply(u):
        s, j = u // PER_PASS, u % PER_PASS
        right = []
        for t in range(COLS // TILE):
            blocks = [wv[inv[(j * 4 + t) * CD + k]] for k in range(CD)]
            right.append(jnp.concatenate(blocks, 0))
        right = jnp.concatenate(right, 1)
        plus = jnp.dot(a[s, 0:128], right, preferred_element_type=F32)
        minus = jnp.dot(a[s, 128:256], right, preferred_element_type=F32)
        d[u] = plus - minus

    def first_pack(u, dims):
        pack(u, 0, [share(u, p, dims)[...] for p in range(8, 16)])

    def middle(u, k, dims):
        count = 16 >> k
        half = count // 2
        pack(u, k, [share(u, p, dims)[...] + unpack(u, k - 1, p) for p in range(half, count)])
        for p in range(half):
            ref = share(u, p, dims)
            ref[...] = ref[...] + unpack(u, k - 1, p)

    def out_ref(u):
        s, j = u // PER_PASS, u % PER_PASS
        col = pl.multiple_of(COLS * j + 256 * xb, 256)
        return held.at[pl.ds(pl.multiple_of(16 * s, 16), 16), pl.ds(col, 256)]

    def last(u, dims):
        total = share(u, 0, dims)[...] + unpack(u, 3, 0)
        out_ref(u)[...] = total.astype(jnp.bfloat16)

    def deliver(u):
        return pltpu.make_async_remote_copy(
            src_ref=out_ref(u), dst_ref=out_ref(u),
            send_sem=ssend.at[u, 4], recv_sem=srecv.at[u, 4],
            device_id=(vrow, opposite), device_id_type=MESH,
        )

    gather_start(0)
    gather_forward(0)
    gather_last(0)
    for c in range(PARTS):
        load_part(c).wait()

    rounds = UNITS // 4

    def turn(it, unused):
        @pl.when((it % 2 == 0) & (it < rounds))
        def _():
            gather_end(it // 2)

            @pl.when(it < rounds - 2)
            def _():
                gather_start(it // 2 + 1)

        @pl.when((it % 2 == 1) & (it < rounds - 2))
        def _():
            gather_forward(it // 2 + 1)

        for r in range(4):
            dims = dims_of(r)
            for k in (4, 3, 2, 1):
                @pl.when((it >= k) & (it < rounds + k))
                def _():
                    u = (it - k) * 4 + r
                    exchange(u, k - 1, dims).wait_recv()
                    if k == 4:
                        last(u, dims)
                        deliver(u).start()
                    else:
                        middle(u, k, dims)
                        exchange(u, k, dims).start()

            @pl.when(it < rounds)
            def _():
                u = it * 4 + r
                multiply(u)
                first_pack(u, dims)
                exchange(u, 0, dims).start()

            if r == 2:
                @pl.when((it % 2 == 1) & (it < rounds - 2))
                def _():
                    gather_last(it // 2 + 1)
        return unused

    lax.fori_loop(0, rounds + 4, turn, 0)

    def finish(u, unused):
        for k in range(4):
            exchange(u, k, [0, 1, 2, 3]).wait_send()
        deliver(u).wait_send()
        s, j = u // PER_PASS, u % PER_PASS
        col = pl.multiple_of(COLS * j + 256 * (1 - xb), 256)
        ref = held.at[pl.ds(pl.multiple_of(16 * s, 16), 16), pl.ds(col, 256)]
        pltpu.make_async_remote_copy(
            src_ref=ref, dst_ref=ref,
            send_sem=ssend.at[u, 4], recv_sem=srecv.at[u, 4],
            device_id=(vrow, opposite), device_id_type=MESH,
        ).wait_recv()
        return unused

    lax.fori_loop(0, UNITS, finish, 0)
    for s in range(PASSES):
        for kind in range(8):
            gather_copy(s, kind).wait_send()

    sign = (1 - 2 * xb).astype(jnp.bfloat16)
    out[...] = held[...] * sign


def per_device(pair_amps, integrals, block_index, block_count):
    slot_ids = jnp.arange(SLOTS, dtype=jnp.int32)
    index = jnp.where(slot_ids < block_count[0, 0], block_index[0, 0], SLOTS)
    hit = index[None, :] == slot_ids[:, None]
    inverse = SLOTS + jnp.sum(jnp.where(hit, slot_ids[None, :] - SLOTS, 0), axis=1)
    messages = [pltpu.VMEM((UNITS, (128 >> k) + 16, 256), jnp.int16) for k in range(4)]
    return pl.pallas_call(
        kernel,
        out_shape=jax.ShapeDtypeStruct((48, 4096), jnp.bfloat16),
        in_specs=[
            pl.BlockSpec(memory_space=pltpu.SMEM),
            pl.BlockSpec(memory_space=pl.ANY),
            pl.BlockSpec(memory_space=pl.ANY),
        ],
        out_specs=pl.BlockSpec(memory_space=pltpu.VMEM),
        scratch_shapes=[
            pltpu.VMEM((SLOTS + 1, TILE, TILE), jnp.bfloat16),
            pltpu.VMEM((PASSES, 256, DEPTH), jnp.bfloat16),
            pltpu.VMEM((UNITS, 128, COLS), F32),
            *messages,
            *messages,
            pltpu.VMEM((48, 4096), jnp.bfloat16),
            pltpu.SemaphoreType.DMA((PARTS,)),
            pltpu.SemaphoreType.DMA((2 * PASSES,)),
            pltpu.SemaphoreType.DMA((PASSES, 8)),
            pltpu.SemaphoreType.DMA((PASSES, 8)),
            pltpu.SemaphoreType.DMA((UNITS, 5)),
            pltpu.SemaphoreType.DMA((UNITS, 5)),
        ],
        compiler_params=pltpu.CompilerParams(
            collective_id=0, has_side_effects=True, vmem_limit_bytes=56 << 20
        ),
        name="ladder",
    )(inverse.astype(jnp.int32), pair_amps, integrals[0, 0])


def solution(mesh):
    placed = (
        P("vrow", "vcol"),
        P("vrow", "vcol", None, None, None),
        P("vrow", "vcol", None),
        P("vrow", "vcol"),
    )
    return jax.shard_map(
        per_device, mesh=mesh, in_specs=placed, out_specs=P("vcol", "vrow"), check_vma=False
    )
```

time: 219 us -> 75.3 us (0.34)
  waiting for transfers between devices: 116 us -> 0 us
  Pallas kernels: 0 us -> 71.2 us
  matrix products: 50 us -> 0 us
  local copies, waits for them, and re-layouts: 34.2 us -> 1.77 us
  between operations: 14.1 us -> 0.66 us
  starting transfers between devices: 2.32 us -> 0 us
    reduce_scatter x1 -> x0, waiting for transfers between devices: 96.9 us -> none  [per_device(): lax.psum_scatter(partial_value, 'vcol', scatter_dimension=0, tiled=True)]
    pallas_call x0 -> x1, Pallas kernels: none -> 71.2 us  [per_device(): pl.pallas_call(kernel, out_shape=jax.ShapeDtypeStruct((48, 4096), jnp.bfl...]
    dot_general x2 -> x0, matrix products: 50 us -> none  [the longest x1 27.6 us: per_device(): jnp.dot(lax.all_gather(pair_amps, 'vrow', axis=0, tiled=True), dense_weig...]
    unnamed x2 -> x1, local copies, waits for them, and re-layouts: 22.6 us -> 1.77 us
    ppermute x1 -> x0, waiting for transfers between devices: 18.4 us -> none  [shifted(): lax.ppermute(array, axis, [(i, (i + by) % size) for i in range(size)])]
    reshape x1 -> x0, local copies, waits for them, and re-layouts: 11.6 us -> none  [per_device(): placed = placed.reshape(ab_tiles, cd_tiles, tile_size, tile_size)]
    ppermute x1 -> x0, starting transfers between devices: 2.28 us -> none  [shifted(): lax.ppermute(array, axis, [(i, (i + by) % size) for i in range(size)])]
  transfers between devices with their start and end apart: 3 -> 0, of which waited for: 2 -> 0; matrix products, arithmetic and copies ran while one was open for 20% -> 0% of each run, Pallas kernels for 0% -> 0%
where the time goes in v1:
time: 75.3 us; the launch traced here: 75.1 us
  Pallas kernels  71.2 us (95%)
  local copies, waits for them, and re-layouts  1.77 us (2%)
  other arithmetic  1.46 us (2%)
    pallas_call x1, Pallas kernels, per_device(): pl.pallas_call(kernel, out_shape=jax.ShapeDtypeStruct((48, 4096), jnp.bfl...  71.2 us
    unnamed x1, local copies, waits for them, and re-layouts  1.77 us

profile of v1, /device:TPU:0, one launch (start us, length us, event | category | flops | bytes accessed | tf_op | source)
XLA Modules:
  0.0 75.1 jit_solution(15256022606912262113)
XLA Ops:
  0.7 0.7 iota_add_fusion
  1.3 0.2 select_reduce_fusion
  1.5 0.6 broadcast_add_fusion.inv
  2.1 71.2 %ladder.1 = bf16[48,4096]{1,0:T(8,128)(2,1)} custom-call(s32[512]{0:T(512)} %broadcast_add_fusion.inv, bf16[96,2048]{1,0:T(8,128)(2,1)} %amps.1, bf16[512,128,128]{2,1,0:T(8,128)(2,1)} %bitcast.4), custom_call_target="tpu_custom_call" | custom-call | tf_op jit(solution)/shard_map/ladder/pallas_call | solution.py:289
  73.3 1.8 %copy.7 = bf16[48,4096]{1,0:T(8,128)(2,1)} copy(bf16[48,4096]{1,0:T(8,128)(2,1)} %ladder.1) | data formatting | bytes 786432

commit v2 on v0

v2 whole, which is shorter than its diff:
```python
import jax
import jax.numpy as jnp
from jax import lax
from jax.experimental import pallas as pl
from jax.experimental.pallas import tpu as pltpu
from jax.sharding import PartitionSpec as P

MESH = pl.DeviceIdType.MESH
F32 = jnp.float32
TILE = 128
SLOTS = 512
CD = 16
DEPTH = CD * TILE
PASSES = 3
COLS = 1024
UNITS = 12
PER_PASS = 4
DIRECT = 3
LAGS = (2, 4, 6)
LEVELS = 32766.0
PARTS = 16


def kernel(
    index, count, amps, w_hbm, out, inv_v, inv, wv, a, d, acc, sent1, got1, sent2, got2, held,
    isem, wsem, asem, gsend, grecv, ssend, srecv,
):
    vrow, vcol = lax.axis_index("vrow"), lax.axis_index("vcol")
    z, core = vrow // 2, vrow % 2
    x, y = vcol // 4, vcol % 4

    per = SLOTS // PARTS

    def load_part(c):
        part, into = pl.ds(c * per, per), pl.ds(1 + c * per, per)
        return pltpu.make_async_copy(w_hbm.at[part], wv.at[into], wsem.at[c])

    def load_rows(s, i):
        return pltpu.make_async_copy(
            amps.at[pl.ds(48 * i + 16 * s, 16)],
            a.at[s, pl.ds(32 * vrow + 16 * i, 16)],
            asem.at[2 * s + i],
        )

    for s in range(PASSES):
        for i in range(2):
            load_rows(s, i).start()

    above, below, across = (vrow + 2) % 8, (vrow + 6) % 8, (vrow + 4) % 8
    sibling = 2 * z + 1 - core
    along_x = [((x + n) % 4) * 4 + y for n in range(4)]
    along_y = [x * 4 + (y + n) % 4 for n in range(4)]

    barrier = pltpu.get_barrier_semaphore()
    peers = [(above, vcol), (below, vcol), (across, vcol), (sibling, vcol)]
    peers += [(vrow, p) for p in along_x[1:] + along_y[1:]]
    for peer in peers:
        pl.semaphore_signal(barrier, inc=1, device_id=peer, device_id_type=MESH)
    wv[0] = jnp.zeros((TILE, TILE), jnp.bfloat16)
    for s in range(PASSES):
        for i in range(2):
            load_rows(s, i).wait()
    pl.semaphore_wait(barrier, len(peers))

    own = 32 * vrow
    from_rows = [own, 32 * below, 32 * above, 32 * across]
    near_rows = [32 * ((sibling + n) % 8) for n in (0, 6, 2, 4)]

    def piece(s, first, target, kind, rows=32):
        ref = a.at[s, pl.ds(pl.multiple_of(first, 16), rows)]
        return pltpu.make_async_remote_copy(
            src_ref=ref, dst_ref=ref,
            send_sem=gsend.at[s, kind], recv_sem=grecv.at[s, kind],
            device_id=(target, vcol), device_id_type=MESH,
        )

    def gather_start(s):
        piece(s, own, above, 1).start()
        piece(s, own, below, 2).start()
        piece(s, own, sibling, 4).start()

    def gather_near(s):
        piece(s, from_rows[1], sibling, 1).wait_recv()
        piece(s, from_rows[1], above, 0, 16).start()
        piece(s, from_rows[1], sibling, 5).start()
        piece(s, from_rows[2], sibling, 2).wait_recv()
        piece(s, from_rows[2] + 16, below, 3, 16).start()
        piece(s, from_rows[2], sibling, 6).start()

    def gather_far(s):
        piece(s, from_rows[3], sibling, 0, 16).wait_recv()
        piece(s, from_rows[3] + 16, sibling, 3, 16).wait_recv()
        piece(s, from_rows[3], sibling, 7).start()

    def gather_end(s):
        for n in range(4):
            piece(s, near_rows[n], sibling, 4 + n).wait_recv()

    def gather_sent(s):
        for n in range(8):
            piece(s, own, sibling, n, 16 if n in (0, 3) else 32).wait_send()

    def message1(u, n, kind, slot=None, rows=272):
        target = (along_x if kind == "x" else along_y)[n]
        slot = n - 1 if slot is None else slot
        part = pl.ds(0, rows)
        return pltpu.make_async_remote_copy(
            src_ref=sent1.at[u, slot, part], dst_ref=got1.at[u, slot, part],
            send_sem=ssend.at[u, slot], recv_sem=srecv.at[u, slot],
            device_id=(vrow, target), device_id_type=MESH,
        )

    def passed_on(u, n, kind):
        return message1(u, n, kind, n, 144)

    def message2(u, n, kind):
        rows = pl.ds(0, 80 if kind == "x" else 144)
        target = (along_y if kind == "x" else along_x)[n]
        slot = 0 if kind == "y" and n == 3 else n - 1
        return pltpu.make_async_remote_copy(
            src_ref=sent2.at[u, slot, rows], dst_ref=got2.at[u, n - 1, rows],
            send_sem=ssend.at[u, 3 + n], recv_sem=srecv.at[u, 3 + n],
            device_id=(vrow, target), device_id_type=MESH,
        )

    def pack(ref, values):
        most = jnp.abs(values[0])
        for value in values[1:]:
            most = jnp.maximum(most, jnp.abs(value))
        most = jnp.maximum(jnp.max(most, axis=0, keepdims=True), 1e-30)
        code = jnp.ceil(jnp.log(most) * 256.0)
        factor = jnp.exp(code * (-1.0 / 256.0)) * LEVELS
        for n, value in enumerate(values):
            q = jnp.round(value * factor).astype(jnp.int32)
            ref[16 * n : 16 * n + 16] = q.astype(jnp.int16)
        n = len(values)
        wide = jnp.broadcast_to(code, (16, TILE)).astype(jnp.int32)
        ref[16 * n : 16 * n + 16] = wide.astype(jnp.int16)

    def unpacked(ref, count):
        code = ref[16 * count : 16 * count + 16].astype(jnp.int32).astype(F32)
        factor = jnp.exp(code * (1.0 / 256.0)) * (1.0 / LEVELS)

        def at(n):
            return ref[16 * n : 16 * n + 16].astype(jnp.int32).astype(F32) * factor

        return at

    def region(u, kind, to):
        pieces = []
        if kind == "x":
            for c in range(4):
                col = pl.multiple_of(512 * (to // 2) + TILE * c, TILE)
                for g in range(4):
                    row = pl.multiple_of(64 * (to % 2) + 16 * g, 16)
                    pieces.append(d.at[u, pl.ds(row, 16), pl.ds(col, TILE)])
        else:
            for half in range(2):
                row = pl.multiple_of(64 * half + 16 * to, 16)
                for c in range(8):
                    pieces.append(d.at[u, pl.ds(row, 16), pl.ds(TILE * c, TILE)])
        return pieces

    def multiply(u):
        s, j = u // PER_PASS, u % PER_PASS

        right = []
        for t in range(COLS // TILE):
            right.append(jnp.concatenate([wv[inv[j, t * CD + k]] for k in range(CD)], 0))
        right = jnp.concatenate(right, 1)
        both = jnp.dot(a[s], right, preferred_element_type=F32)
        d[u] = both[:128] - both[128:]

    def first(u, kind):
        me = x if kind == "x" else y
        for n in (2, 1, 3):
            pieces = region(u, kind, (me + n) % 4)
            pack(sent1.at[u, n - 1], [p[...] for p in pieces])
            message1(u, n, kind).start()

    def first_ring(u, kind):
        me = x if kind == "x" else y
        far = region(u, kind, (me + 2) % 4)
        right, left = region(u, kind, (me + 1) % 4), region(u, kind, (me + 3) % 4)
        pack(sent1.at[u, 0], [p[...] for p in far[:8] + right[8:]])
        message1(u, 1, kind).start()
        pack(sent1.at[u, 2], [p[...] for p in far[8:] + left[:8]])
        message1(u, 3, kind).start()

    def relay(u, kind):
        me = x if kind == "x" else y
        message1(u, 1, kind).wait_recv()
        got = unpacked(got1.at[u, 0], 16)
        right = region(u, kind, (me + 1) % 4)[:8]
        pack(sent1.at[u, 1], [p[...] + got(n) for n, p in enumerate(right)])
        passed_on(u, 1, kind).start()
        message1(u, 3, kind).wait_recv()
        got = unpacked(got1.at[u, 2], 16)
        left = region(u, kind, (me + 3) % 4)[8:]
        pack(sent1.at[u, 3], [p[...] + got(n) for n, p in enumerate(left)])
        passed_on(u, 3, kind).start()

    def second_ring(u, kind):
        passed_on(u, 1, kind).wait_recv()
        passed_on(u, 3, kind).wait_recv()
        plain = [unpacked(got1.at[u, 2], 16), unpacked(got1.at[u, 0], 16)]
        summed = [unpacked(got1.at[u, 1], 8), unpacked(got1.at[u, 3], 8)]
        for n, ref in enumerate(region(u, kind, x if kind == "x" else y)):
            h = n // 8
            acc[u, 16 * n : 16 * n + 16] = ref[...] + plain[h](n % 8 + 8) + summed[h](n % 8)
        send_second(u, kind)

    def second(u, kind):
        for n in (1, 3, 2):
            message1(u, n, kind).wait_recv()
        got = [unpacked(got1.at[u, n], 16) for n in range(3)]
        for n, ref in enumerate(region(u, kind, x if kind == "x" else y)):
            acc[u, 16 * n : 16 * n + 16] = ref[...] + (got[0](n) + got[1](n)) + got[2](n)
        send_second(u, kind)

    def send_second(u, kind):
        if kind == "x":
            for n in (2, 1, 3):
                row = 16 * ((y + n) % 4)
                values = []
                for c in range(4):
                    values.append(acc[u, pl.ds(pl.multiple_of(64 * c + row, 16), 16)])
                pack(sent2.at[u, n - 1], values)
                message2(u, n, kind).start()
        else:
            for n in (2, 1):
                row = 128 * ((x + n) % 2)
                values = []
                for c in range(8):
                    values.append(acc[u, pl.ds(pl.multiple_of(row + 16 * c, 16), 16)])
                pack(sent2.at[u, n - 1], values)
                message2(u, n, kind).start()
                if n == 1:
                    message2(u, 3, kind).start()

    def held_ref(u, first_col, cols):
        s, j = u // PER_PASS, u % PER_PASS
        col = pl.multiple_of(COLS * j + first_col, TILE)
        return held.at[pl.ds(pl.multiple_of(16 * s, 16), 16), pl.ds(col, cols)]

    def third(u, kind):
        for n in (1, 3, 2):
            message2(u, n, kind).wait_recv()
        count = 4 if kind == "x" else 8
        got = [unpacked(got2.at[u, n], count) for n in range(3)]
        for c in range(count):
            if kind == "x":
                row, col = 64 * c + 16 * y, 512 * (x // 2) + TILE * c
            else:
                row, col = 128 * (x % 2) + 16 * c, TILE * c
            mine = acc[u, pl.ds(pl.multiple_of(row, 16), 16)]
            total = mine + (got[0](c) + got[1](c)) + got[2](c)
            held_ref(u, col, TILE)[...] = total.astype(jnp.bfloat16)
        if kind == "x":
            deliver(u, x // 2).start()

    def deliver(u, half):
        ref = held_ref(u, 512 * half, 512)
        return pltpu.make_async_remote_copy(
            src_ref=ref, dst_ref=ref,
            send_sem=ssend.at[u, 7], recv_sem=srecv.at[u, 7],
            device_id=(vrow, along_x[2]), device_id_type=MESH,
        )

    gather_start(0)
    for c in range(PARTS):
        load_part(c).start()
    slots = lax.broadcasted_iota(jnp.int32, (TILE, TILE), 0)
    pairs = lax.broadcasted_iota(jnp.int32, (TILE, TILE), 1)
    live = count[0, 0]
    for g in range(4):
        found = jnp.zeros((1, TILE), jnp.int32)
        for q in range(4):
            row = jnp.broadcast_to(index[q : q + 1], (TILE, TILE))
            hit = (jnp.transpose(row) == pairs + TILE * g) & (slots < live - TILE * q)
            most = jnp.max(jnp.where(hit, slots + (TILE * q + 1), 0), axis=0, keepdims=True)
            found = jnp.maximum(found, most)
        inv_v[g : g + 1] = found
    to_scalar = pltpu.make_async_copy(inv_v, inv, isem)
    to_scalar.start()
    gather_near(0)
    gather_start(1)
    gather_far(0)
    gather_end(0)
    to_scalar.wait()
    for c in range(PARTS):
        load_part(c).wait()

    ring = UNITS - DIRECT

    def of_kind(u, step):
        @pl.when(u % 3 == 1)
        def _():
            step(u, "x")

        @pl.when(u % 3 != 1)
        def _():
            step(u, "y")

    def sends_done(u, kind):
        for n in (1, 3):
            message1(u, n, kind).wait_send()

        @pl.when(u < ring)
        def _():
            for n in (1, 3):
                passed_on(u, n, kind).wait_send()

        @pl.when(u >= ring)
        def _():
            message1(u, 2, kind).wait_send()

    def turn(t, unused):
        @pl.when(t < UNITS)
        def _():
            s, step = t // PER_PASS, t % PER_PASS

            @pl.when((step == 0) & (s > 0))
            def _():
                gather_end(s)

            multiply(t)

            @pl.when(t < ring)
            def _():
                of_kind(t, first_ring)

            @pl.when(t >= ring)
            def _():
                of_kind(t, first)

        @pl.when(t == 0)
        def _():
            gather_near(1)
            gather_start(2)

        @pl.when(t == 2)
        def _():
            gather_far(1)

        @pl.when(t == 3)
        def _():
            gather_near(2)

        @pl.when(t == 5)
        def _():
            gather_far(2)

        u = t - LAGS[0]

        @pl.when((u >= 0) & (u < ring))
        def _():
            of_kind(u, relay)

        @pl.when((u >= ring) & (u < UNITS))
        def _():
            of_kind(u, second)

        u = t - LAGS[1]

        @pl.when((u >= 0) & (u < ring))
        def _():
            of_kind(u, second_ring)

        @pl.when((u >= ring) & (u < UNITS))
        def _():
            of_kind(u, third)

        u = t - LAGS[2]

        @pl.when((u >= 0) & (u < ring))
        def _():
            of_kind(u, third)

        @pl.when(u >= 0)
        def _():
            of_kind(u, sends_done)

        return unused

    turns = max(UNITS + LAGS[1], ring + LAGS[2])
    lax.fori_loop(0, turns, turn, 0)

    for u in range(turns - LAGS[2], UNITS):
        sends_done(u, "x" if u % 3 == 1 else "y")

    def finish(u, unused):
        def sent(u, kind):
            for n in (1, 2, 3):
                message2(u, n, kind).wait_send()
            if kind == "x":
                deliver(u, x // 2).wait_send()
                deliver(u, 1 - x // 2).wait_recv()

        of_kind(u, sent)
        return unused

    lax.fori_loop(0, UNITS, finish, 0)
    for s in range(PASSES):
        gather_sent(s)

    sign = (1 - 2 * (x // 2)).astype(jnp.bfloat16)
    out[...] = held[...] * sign


def per_device(pair_amps, integrals, block_index, block_count):
    first_phase = pltpu.VMEM((UNITS, 4, 272, TILE), jnp.int16)
    second_phase = pltpu.VMEM((UNITS, 3, 144, TILE), jnp.int16)
    return pl.pallas_call(
        kernel,
        out_shape=jax.ShapeDtypeStruct((48, 4096), jnp.bfloat16),
        in_specs=[
            pl.BlockSpec(memory_space=pltpu.VMEM),
            pl.BlockSpec(memory_space=pltpu.SMEM),
            pl.BlockSpec(memory_space=pl.ANY),
            pl.BlockSpec(memory_space=pl.ANY),
        ],
        out_specs=pl.BlockSpec(memory_space=pltpu.VMEM),
        scratch_shapes=[
            pltpu.VMEM((4, TILE), jnp.int32),
            pltpu.SMEM((4, TILE), jnp.int32),
            pltpu.VMEM((SLOTS + 1, TILE, TILE), jnp.bfloat16),
            pltpu.VMEM((PASSES, 256, DEPTH), jnp.bfloat16),
            pltpu.VMEM((UNITS, 128, COLS), F32),
            pltpu.VMEM((UNITS, 256, TILE), F32),
            first_phase,
            first_phase,
            second_phase,
            second_phase,
            pltpu.VMEM((48, 4096), jnp.bfloat16),
            pltpu.SemaphoreType.DMA,
            pltpu.SemaphoreType.DMA((PARTS,)),
            pltpu.SemaphoreType.DMA((2 * PASSES,)),
            pltpu.SemaphoreType.DMA((PASSES, 8)),
            pltpu.SemaphoreType.DMA((PASSES, 8)),
            pltpu.SemaphoreType.DMA((UNITS, 8)),
            pltpu.SemaphoreType.DMA((UNITS, 8)),
        ],
        compiler_params=pltpu.CompilerParams(
            collective_id=0, has_side_effects=True, vmem_limit_bytes=56 << 20
        ),
        name="ladder",
    )(block_index.reshape(4, TILE), block_count, pair_amps, integrals[0, 0])


def solution(mesh):
    placed = (
        P("vrow", "vcol"),
        P("vrow", "vcol", None, None, None),
        P("vrow", "vcol", None),
        P("vrow", "vcol"),
    )
    return jax.shard_map(
        per_device, mesh=mesh, in_specs=placed, out_specs=P("vcol", "vrow"), check_vma=False
    )
```

time: 219 us -> 60.4 us (0.28)
  waiting for transfers between devices: 116 us -> 0 us
  Pallas kernels: 0 us -> 57.7 us
  matrix products: 50 us -> 0 us
  local copies, waits for them, and re-layouts: 34.2 us -> 1.77 us
  between operations: 14.1 us -> 0.66 us
  starting transfers between devices: 2.32 us -> 0 us
    reduce_scatter x1 -> x0, waiting for transfers between devices: 96.9 us -> none  [per_device(): lax.psum_scatter(partial_value, 'vcol', scatter_dimension=0, tiled=True)]
    pallas_call x0 -> x1, Pallas kernels: none -> 57.7 us  [per_device(): pl.pallas_call(kernel, out_shape=jax.ShapeDtypeStruct((48, 4096), jnp.bfl...]
    dot_general x2 -> x0, matrix products: 50 us -> none  [the longest x1 27.6 us: per_device(): jnp.dot(lax.all_gather(pair_amps, 'vrow', axis=0, tiled=True), dense_weig...]
    unnamed x2 -> x1, local copies, waits for them, and re-layouts: 22.6 us -> 1.77 us
    ppermute x1 -> x0, waiting for transfers between devices: 18.4 us -> none  [shifted(): lax.ppermute(array, axis, [(i, (i + by) % size) for i in range(size)])]
    reshape x1 -> x0, local copies, waits for them, and re-layouts: 11.6 us -> none  [per_device(): placed = placed.reshape(ab_tiles, cd_tiles, tile_size, tile_size)]
    ppermute x1 -> x0, starting transfers between devices: 2.28 us -> none  [shifted(): lax.ppermute(array, axis, [(i, (i + by) % size) for i in range(size)])]
  transfers between devices with their start and end apart: 3 -> 0, of which waited for: 2 -> 0; matrix products, arithmetic and copies ran while one was open for 20% -> 0% of each run, Pallas kernels for 0% -> 0%
where the time goes in v2:
time: 60.4 us; the launch traced here: 60.1 us
  Pallas kernels  57.7 us (96%)
  local copies, waits for them, and re-layouts  1.77 us (3%)
  between operations  0.66 us (1%)
    pallas_call x1, Pallas kernels, per_device(): pl.pallas_call(kernel, out_shape=jax.ShapeDtypeStruct((48, 4096), jnp.bfl...  57.7 us
    unnamed x1, local copies, waits for them, and re-layouts  1.77 us

profile of v2, /device:TPU:0, one launch (start us, length us, event | category | flops | bytes accessed | tf_op | source)
XLA Modules:
  0.0 60.1 jit_solution(3588932972416623295)
XLA Ops:
  0.7 57.7 %ladder.1 = bf16[48,4096]{1,0:T(8,128)(2,1)} custom-call(s32[4,128]{1,0:T(4,128)} %bitcast.3, s32[1,1]{1,0:T(1,128)S(6)} %copy.6.count, bf16[96,2048]{1,0:T(8,128)(2,1)} %amps.1, bf16[512,128,128]{2,1,0:T(8,128)(2,1)} %bitcast.2), custom_call_target="tpu_custom_call" | custom-call | tf_op jit(solution)/shard_map/ladder/pallas_call | solution.py:414
  58.3 1.8 %copy.7 = bf16[48,4096]{1,0:T(8,128)(2,1)} copy(bf16[48,4096]{1,0:T(8,128)(2,1)} %ladder.1) | data formatting | bytes 786432
